TPU v7x, 256 devices: a whole 4x4x8 slice. The times are simulated.
256 devices in a mesh: seq: 8 (over y_hi, x), row: 8 (over z), col: 4 (over y_lo, core).
Axes of the slice: x: 4, y: 4 (y_hi: 2, y_lo: 2; y = y_hi * 2 + y_lo), z: 8, core: 2. Of those that a mesh axis runs over, the one named last changes fastest.
Arguments:
- alignment: int32 [32768, 256], P('seq'), may hold values from 0 to 20, as said below
- cluster_sizes: int32 [32768], P('seq'), may hold values from 1 to 32, as said below
- block_inverse: float32 [128, 128], replicated, may hold values from -12 to 12
Outputs:
- couplings: float32 [5120, 5120], P(('seq', 'row'), 'col')
Inputs may be any that keep to these rules, and one draw needn't show every extreme that they name: `alignment`: the value 20 marks a gap. `cluster_sizes`: every cluster size is a power of two.
All inputs are finite; a program needn't handle non-finite values.
Results may differ from a plain program's by a relative error of at most 0.0003.
Values sent between devices are 32-bit elements; how exact they have to be, the bound alone decides.
A program may use at most 64 MiB of HBM per device.

v0:
```python
import jax
import jax.numpy as jnp
from jax import lax
from jax.sharding import PartitionSpec as P

Q = 20
POS = 256
PANEL = 128
PSEUDOCOUNT = 0.5


def spread(value, axis, source):
    kept = jnp.where(lax.axis_index(axis) == source, value, 0).astype(value.dtype)
    return lax.psum(kept, axis)


def one_hot_states(states):
    levels = lax.broadcasted_iota(jnp.int32, (1, 1, Q), 2)
    matches = (states[:, :, None] == levels).astype(jnp.bfloat16)
    return matches.reshape(states.shape[0], states.shape[1] * Q)


def covariance_block(pair_block, row_margin, col_margin, weight_total, row_start, col_start):
    row_freq = (1.0 - PSEUDOCOUNT) * row_margin / weight_total + PSEUDOCOUNT / Q
    col_freq = (1.0 - PSEUDOCOUNT) * col_margin / weight_total + PSEUDOCOUNT / Q
    shape_rc = pair_block.shape
    row_ids = row_start + lax.broadcasted_iota(jnp.int32, shape_rc, 0)
    col_ids = col_start + lax.broadcasted_iota(jnp.int32, shape_rc, 1)
    same_pos = row_ids // Q == col_ids // Q
    prior = jnp.where(
        same_pos, jnp.where(row_ids == col_ids, PSEUDOCOUNT / Q, 0.0), PSEUDOCOUNT / (Q * Q)
    )
    joint = (1.0 - PSEUDOCOUNT) * pair_block / weight_total + prior
    return joint - row_freq[:, None] * col_freq[None, :]


def accumulate_pairs(row_states, column_sets, span_widths, seq_weight):
    local_seqs = row_states.shape[0]
    block_rows = min(local_seqs, 1024)
    count_blocks = local_seqs // block_rows
    row_width = row_states.shape[1] * Q

    def blocked(states):
        return states.reshape(count_blocks, block_rows, states.shape[1])

    def add_block(running, block_item):
        pair_totals, row_margin, column_margins = running
        row_block, weight_block, column_blocks = block_item
        row_hot = one_hot_states(row_block)
        weighted = row_hot * weight_block[:, None]
        new_pairs = []
        new_margins = []
        for pair_total, margin_total, states_block, span_width in zip(
            pair_totals, column_margins, column_blocks, span_widths
        ):
            column_hot = one_hot_states(states_block)
            new_pairs.append(
                pair_total
                + lax.dot_general(
                    weighted,
                    column_hot,
                    (((0,), (0,)), ((), ())),
                    preferred_element_type=jnp.float32,
                )
            )
            new_margins.append(
                margin_total + jnp.dot(weight_block, column_hot, preferred_element_type=jnp.float32)
            )
        row_margin = row_margin + jnp.dot(weight_block, row_hot, preferred_element_type=jnp.float32)
        return ((tuple(new_pairs), row_margin, tuple(new_margins)), None)

    initial = (
        tuple((jnp.zeros((row_width, span_width), jnp.float32) for span_width in span_widths)),
        jnp.zeros((row_width,), jnp.float32),
        tuple((jnp.zeros((span_width,), jnp.float32) for span_width in span_widths)),
    )
    block_items = (
        blocked(row_states),
        seq_weight.reshape(count_blocks, block_rows),
        tuple((blocked(states) for states in column_sets)),
    )
    result, unused = lax.scan(add_block, initial, block_items)
    return result


def shards(alignment, cluster_sizes, block_inverse):
    seq_count = lax.axis_size("seq")
    row_count = lax.axis_size("row")
    col_count = lax.axis_size("col")
    seq_index = lax.axis_index("seq")
    row_index = lax.axis_index("row")
    col_index = lax.axis_index("col")
    local_seqs = alignment.shape[0]
    row_positions = POS // (seq_count * row_count)
    col_positions = POS // col_count
    block_features = row_positions * Q
    col_features = col_positions * Q
    seq_weight = (1.0 / cluster_sizes.astype(jnp.float32)).astype(jnp.bfloat16)
    grouped = alignment.reshape(local_seqs, seq_count, row_count, row_positions)
    row_states = lax.dynamic_slice_in_dim(grouped, row_index, 1, 2).reshape(
        local_seqs, seq_count * row_positions
    )
    col_states = lax.dynamic_slice_in_dim(alignment, col_index * col_positions, col_positions, 1)
    weight_local = jnp.sum(seq_weight.astype(jnp.float32))
    row_start = (seq_index * row_count + row_index) * block_features
    col_start = col_index * col_features
    pair_totals, row_margin, column_margins = accumulate_pairs(
        row_states, (col_states,), (col_features,), seq_weight
    )
    weight_total, row_margin, col_margin = lax.psum(
        (weight_local, row_margin, column_margins[0]), "seq"
    )
    pair_tile = lax.psum_scatter(pair_totals[0], "seq", scatter_dimension=0, tiled=True)
    own_margin = lax.dynamic_slice_in_dim(row_margin, seq_index * block_features, block_features)
    cov_tile = covariance_block(
        pair_tile, own_margin, col_margin, weight_total, row_start, col_start
    )
    panel_rows = spread(cov_tile[:, :PANEL], "col", 0)
    sym_inverse = 0.5 * (block_inverse + block_inverse.T)
    left_factor = jnp.dot(panel_rows, sym_inverse, precision=lax.Precision.HIGHEST)
    whole_panel = lax.all_gather(panel_rows, ("seq", "row"), axis=0, tiled=True)
    panel_cols = lax.dynamic_slice_in_dim(whole_panel, col_start, col_features, 0)
    update = lax.dot_general(
        left_factor, panel_cols, (((1,), (1,)), ((), ())), precision=lax.Precision.HIGHEST
    )
    return -Q * (cov_tile - update)


def solution(mesh):
    in_specs = (P("seq", None), P("seq"), P())
    out_specs = P(("seq", "row"), "col")
    return jax.shard_map(shards, mesh=mesh, in_specs=in_specs, out_specs=out_specs, check_vma=False)
```

profile of v0, /device:TPU:6, one launch (start us, length us, event | category | flops | bytes accessed | tf_op | source)
XLA Modules:
  0.0 306.2 jit_solution(9124577262664192869)
XLA Ops:
  6.5 5.6 %copy.9 = s32[4096,256]{0,1:T(8,128)} copy(s32[4096,256]{1,0:T(8,128)} %param.5) | data formatting | bytes 8388608 | tf_op args[0]
  12.1 2.2 constant_dynamic-slice_fusion.4
  14.9 5.2 %reshape.159 = s32[4096,8,8,4]{0,3,2,1:T(4,128)} reshape(s32[4096,256]{0,1:T(8,128)} %copy.9) | data formatting | bytes 8388608 | tf_op jit(solution)/shard_map/reshape | solution.py:99
  20.1 1.1 constant_dynamic-slice_fusion.5
  21.2 1.2 reshape_reshape.3
  23.1 51.7 %while.15 = (s32[]{:T(128)}, f32[640,1280]{1,0:T(8,128)}, f32[640]{0:T(1024)S(1)}, f32[1280]{0:T(1024)S(1)}, s32[4,1024,32]{1,0,2:T(4,128)}, /*index=5*/bf16[4,1...) while((s32[]{:T(128)}, f32[640,1280]{1,0:T(8,128)}, f32[640]{0:T(1024)S(1)}, ...), condition=%wide.region_1.2_spmd.clone, body=%wide.region_0.0_spmd.clone.sunk | while | flops 1686572800 | bytes 30978228 | solution.py:82
  23.2 1.5 constant_dynamic-slice_fusion.7
  25.2 1.2 mul.117
  26.5 0.9 iota_compare_fusion.4
  28.2 5.0 %convolution_add_fusion.2 = f32[640,1280]{1,0:T(8,128)} fusion(bf16[1024,640]{0,1:T(8,128)(2,1)} %mul.117, pred[1024,1280]{0,1:T(32,128)(4,1)S(1)} %eq.120, f32[640,1280]{1,0:T(8,128)} %get-tuple-element.161, pred[]{:T(512)S(6)} %compare.3), kind=kOutput, calls=%fused_computation.1.clone.1 | convolution fusion | flops 1679360000 | bytes 9175041 | tf_op jit(solution)/shard_map/while/body/eval_jaxpr/dot_general | solution.py:59
  33.2 0.8 convolution_reduce_fusion.5
  35.4 1.5 constant_dynamic-slice_fusion.7
  37.4 1.2 mul.117
  38.7 0.9 iota_compare_fusion.4
  40.3 6.0 %convolution_add_fusion.2 = f32[640,1280]{1,0:T(8,128)} fusion(bf16[1024,640]{0,1:T(8,128)(2,1)} %mul.117, pred[1024,1280]{0,1:T(32,128)(4,1)S(1)} %eq.120, f32[640,1280]{1,0:T(8,128)} %get-tuple-element.161, pred[]{:T(512)S(6)} %compare.3), kind=kOutput, calls=%fused_computation.1.clone.1 | convolution fusion | flops 1679360000 | bytes 9175041 | tf_op jit(solution)/shard_map/while/body/eval_jaxpr/dot_general | solution.py:59
  46.4 0.8 convolution_reduce_fusion.5
  48.5 1.5 constant_dynamic-slice_fusion.7
  50.6 1.2 mul.117
  51.8 0.9 iota_compare_fusion.4
  53.5 6.0 %convolution_add_fusion.2 = f32[640,1280]{1,0:T(8,128)} fusion(bf16[1024,640]{0,1:T(8,128)(2,1)} %mul.117, pred[1024,1280]{0,1:T(32,128)(4,1)S(1)} %eq.120, f32[640,1280]{1,0:T(8,128)} %get-tuple-element.161, pred[]{:T(512)S(6)} %compare.3), kind=kOutput, calls=%fused_computation.1.clone.1 | convolution fusion | flops 1679360000 | bytes 9175041 | tf_op jit(solution)/shard_map/while/body/eval_jaxpr/dot_general | solution.py:59
  59.6 0.8 convolution_reduce_fusion.5
  61.7 1.5 constant_dynamic-slice_fusion.7
  63.8 1.2 mul.117
  65.0 0.9 iota_compare_fusion.4
  66.7 6.0 %convolution_add_fusion.2 = f32[640,1280]{1,0:T(8,128)} fusion(bf16[1024,640]{0,1:T(8,128)(2,1)} %mul.117, pred[1024,1280]{0,1:T(32,128)(4,1)S(1)} %eq.120, f32[640,1280]{1,0:T(8,128)} %get-tuple-element.161, pred[]{:T(512)S(6)} %compare.3), kind=kOutput, calls=%fused_computation.1.clone.1 | convolution fusion | flops 1679360000 | bytes 9175041 | tf_op jit(solution)/shard_map/while/body/eval_jaxpr/dot_general | solution.py:59
  75.0 36.3 %all-reduce = (f32[1280]{0:T(1024)S(1)}, f32[]{:T(128)}, f32[640]{0:T(1024)S(1)}) all-reduce(f32[1280]{0:T(1024)S(1)} %get-tuple-element.46, f32[]{:T(128)} %get-tuple-element.102, f32[640]{0:T(1024)S(1)} %get-tuple-element.45), channel_id=1, replica_groups=mesh['seq'=8,'row'=8,'col'=4] {'seq'}, use_global_device_ids=true, to_apply=%region_6.7 | all-reduce | flops 1921 | bytes 15368 | tf_op jit(solution)/shard_map/psum | solution.py:110
  112.7 51.2 %reduce-scatter.2.cloned.1.call-done = f32[80,1280]{1,0:T(8,128)} async-done(((f32[640,1280]{1,0:T(8,128)}), f32[80,1280]{1,0:T(8,128)}) %reduce-scatter.2.cloned.1.call-update) | async-done | bytes 409616 | tf_op jit(solution)/shard_map/reduce_scatter | solution.py:113
  163.9 1.8 multiply_subtract_fusion
  165.8 11.4 %psum.31 = f32[80,128]{1,0:T(8,128)} all-reduce(f32[80,128]{1,0:T(8,128)S(1)} %slice_select_fusion), channel_id=1, replica_groups=mesh['seq'=8,'row'=8,'col'=4] {'col'}, use_global_device_ids=true, to_apply=%region_7.8 | all-reduce | flops 10240 | bytes 81920 | tf_op jit(solution)/shard_map/psum | solution.py:14
  177.3 1.0 fusion.6
  178.3 118.5 %all-gather.2.cloned.1.call-done = f32[5120,128]{1,0:T(8,128)} async-done(((f32[80,128]{1,0:T(8,128)}), f32[5120,128]{1,0:T(8,128)}) %all-gather.2.cloned.1.call-update) | async-done | bytes 2621456 | tf_op jit(solution)/shard_map/all_gather | solution.py:121
  296.8 2.6 fusion.3
  (81 shorter events, 13.8 us)
Async XLA Ops:
  6.5 157.4 %reduce-scatter.2.cloned.1.call-start = ((), (), s32[]{:S(2)}) async-start(), calls=%async_computation.1 | async-start | bytes 3686400 | tf_op jit(solution)/shard_map/reduce_scatter | solution.py:113
  20.1 2.3 copy-start.3
  23.1 3.3 %copy-start = (s32[4,1024,64]{1,2,0:T(8,128)}, s32[4,1024,64]{1,2,0:T(8,128)S(1)}, u32[]{:S(2)}) copy-start(s32[4,1024,64]{1,2,0:T(8,128)S(1)} %get-tuple-element.175) | copy-start | bytes 3145732 | tf_op jit(solution)/shard_map/while
  33.2 2.1 copy-start.1
  35.3 3.3 %copy-start = (s32[4,1024,64]{1,2,0:T(8,128)}, s32[4,1024,64]{1,2,0:T(8,128)S(1)}, u32[]{:S(2)}) copy-start(s32[4,1024,64]{1,2,0:T(8,128)S(1)} %get-tuple-element.175) | copy-start | bytes 3145732 | tf_op jit(solution)/shard_map/while
  46.4 2.1 copy-start.1
  48.5 3.3 %copy-start = (s32[4,1024,64]{1,2,0:T(8,128)}, s32[4,1024,64]{1,2,0:T(8,128)S(1)}, u32[]{:S(2)}) copy-start(s32[4,1024,64]{1,2,0:T(8,128)S(1)} %get-tuple-element.175) | copy-start | bytes 3145732 | tf_op jit(solution)/shard_map/while
  59.6 2.1 copy-start.1
  61.7 3.3 %copy-start = (s32[4,1024,64]{1,2,0:T(8,128)}, s32[4,1024,64]{1,2,0:T(8,128)S(1)}, u32[]{:S(2)}) copy-start(s32[4,1024,64]{1,2,0:T(8,128)S(1)} %get-tuple-element.175) | copy-start | bytes 3145732 | tf_op jit(solution)/shard_map/while
  72.8 2.1 copy-start.1
  74.9 102.3 %copy-start.2 = (f32[128,128]{1,0:T(8,128)S(1)}, f32[128,128]{1,0:T(8,128)}, u32[]{:S(2)}) copy-start(f32[128,128]{1,0:T(8,128)} %param.7) | copy-start | bytes 196612
  74.9 221.8 %all-gather.2.cloned.1.call-start = ((), (), s32[]{:S(2)}) async-start(), calls=%async_computation.2 | async-start | bytes 2662400 | tf_op jit(solution)/shard_map/all_gather | solution.py:121
Sparse Core Ops, SparseCore 0:
  75.0 88.8 reduce-scatter.1
  177.3 119.4 all-gather.1
where the time goes:
time: 307 us; the launch traced here: 306 us
  waiting for transfers between devices  170 us (55%)
  blocking collectives  47.6 us (16%)
  matrix products  31.8 us (10%)
  local copies, waits for them, and re-layouts  31.7 us (10%)
  between operations  13.5 us (4%)
  other arithmetic  11.4 us (4%)
    all_gather x1, waiting for transfers between devices, shards(): whole_panel = lax.all_gather(panel_rows, ('seq', 'row'), axis=0, tiled=True)  118 us
    reduce_scatter x1, waiting for transfers between devices, shards(): lax.psum_scatter(pair_totals[0], 'seq', scatter_dimension=0, tiled=True)  51.2 us
    psum x1, blocking collectives, shards(): lax.psum((weight_local, row_margin, column_margins[0]), 'seq')  36.3 us
    dot_general x4, matrix products, add_block(): lax.dot_general(weighted, column_hot, (((0,), (0,)), ((), ())), preferred...  23.1 us
    psum x1, blocking collectives, spread(): return lax.psum(kept, axis)  11.4 us
    dynamic_slice x12, local copies, waits for them, and re-layouts, accumulate_pairs(): result, unused = lax.scan(add_block, initial, block_items)  6.38 us
    unnamed x7, local copies, waits for them, and re-layouts  6.29 us
  transfers between devices with their start and end apart: 2, of which 2 were waited for; matrix products, arithmetic and copies ran while one was open for 1% of the time, Pallas kernels for 0%

commit v1 on v0

--- a/solution.py
+++ b/solution.py
@@ -2,6 +2,7 @@
 import jax.numpy as jnp
 from jax import lax
 from jax.sharding import PartitionSpec as P
+from jax.lax import all_to_all, axis_size
 
 Q = 20
 POS = 256
@@ -118,7 +119,9 @@
     panel_rows = spread(cov_tile[:, :PANEL], "col", 0)
     sym_inverse = 0.5 * (block_inverse + block_inverse.T)
     left_factor = jnp.dot(panel_rows, sym_inverse, precision=lax.Precision.HIGHEST)
-    whole_panel = lax.all_gather(panel_rows, ("seq", "row"), axis=0, tiled=True)
+    upper = jnp.stack(axis_size(("seq", "row")) * [panel_rows])
+    raw_out = all_to_all(upper, ("seq", "row"), 0, 0)
+    whole_panel = jnp.concatenate(raw_out, 0)
     panel_cols = lax.dynamic_slice_in_dim(whole_panel, col_start, col_features, 0)
     update = lax.dot_general(
         left_factor, panel_cols, (((1,), (1,)), ((), ())), precision=lax.Precision.HIGHEST

time: 307 us -> 262 us (0.85)
  waiting for transfers between devices: 170 us -> 114 us
  starting transfers between devices: 0.04 us -> 10.4 us
    all_gather x1 -> x0, waiting for transfers between devices: 118 us -> none  [shards(): whole_panel = lax.all_gather(panel_rows, ('seq', 'row'), axis=0, tiled=True)]
    all_to_all x0 -> x1, waiting for transfers between devices: none -> 62.6 us  [shards(): raw_out = all_to_all(upper, ('seq', 'row'), 0, 0)]
    all_to_all x0 -> x1, starting transfers between devices: none -> 10.4 us  [shards(): raw_out = all_to_all(upper, ('seq', 'row'), 0, 0)]
where the time goes in v1:
time: 262 us; the launch traced here: 260 us
  waiting for transfers between devices  114 us (44%)
  blocking collectives  47.1 us (18%)
  local copies, waits for them, and re-layouts  33.4 us (13%)
  matrix products  29.9 us (11%)
  between operations  13.5 us (5%)
  other arithmetic  11.4 us (4%)
  starting transfers between devices  10.4 us (4%)
    all_to_all x1, waiting for transfers between devices, shards(): raw_out = all_to_all(upper, ('seq', 'row'), 0, 0)  62.6 us
    reduce_scatter x1, waiting for transfers between devices, shards(): lax.psum_scatter(pair_totals[0], 'seq', scatter_dimension=0, tiled=True)  51.2 us
    psum x1, blocking collectives, shards(): lax.psum((weight_local, row_margin, column_margins[0]), 'seq')  36.3 us
    dot_general x4, matrix products, add_block(): lax.dot_general(weighted, column_hot, (((0,), (0,)), ((), ())), preferred...  23.1 us
    psum x1, blocking collectives, spread(): return lax.psum(kept, axis)  10.8 us
    all_to_all x1, starting transfers between devices, shards(): raw_out = all_to_all(upper, ('seq', 'row'), 0, 0)  10.4 us
    dynamic_slice x12, local copies, waits for them, and re-layouts, accumulate_pairs(): result, unused = lax.scan(add_block, initial, block_items)  6.38 us
    unnamed x7, local copies, waits for them, and re-layouts  6.29 us
  transfers between devices with their start and end apart: 2, of which 2 were waited for; matrix products, arithmetic and copies ran while one was open for 1% of the time, Pallas kernels for 0%

profile of v1, /device:TPU:6, one launch (start us, length us, event | category | flops | bytes accessed | tf_op | source)
XLA Modules:
  0.0 260.0 jit_solution(16580192273080622342)
XLA Ops:
  6.5 5.6 %copy.9 = s32[4096,256]{0,1:T(8,128)} copy(s32[4096,256]{1,0:T(8,128)} %param.5) | data formatting | bytes 8388608 | tf_op args[0]
  12.1 2.2 constant_dynamic-slice_fusion.4
  15.0 5.2 %reshape.164 = s32[4096,8,8,4]{0,3,2,1:T(4,128)} reshape(s32[4096,256]{0,1:T(8,128)} %copy.9) | data formatting | bytes 8388608 | tf_op jit(solution)/shard_map/reshape | solution.py:100
  20.1 1.1 constant_dynamic-slice_fusion.5
  21.2 1.2 reshape_reshape.3
  23.1 51.7 %while.15 = (s32[]{:T(128)}, f32[640,1280]{1,0:T(8,128)}, f32[640]{0:T(1024)S(1)}, f32[1280]{0:T(1024)S(1)}, s32[4,1024,32]{1,0,2:T(4,128)}, /*index=5*/bf16[4,1...) while((s32[]{:T(128)}, f32[640,1280]{1,0:T(8,128)}, f32[640]{0:T(1024)S(1)}, ...), condition=%wide.region_1.2_spmd.clone, body=%wide.region_0.0_spmd.clone.sunk | while | flops 1686572800 | bytes 30978228 | solution.py:83
  23.2 1.5 constant_dynamic-slice_fusion.7
  25.2 1.2 mul.117
  26.5 0.9 iota_compare_fusion.4
  28.2 5.0 %convolution_add_fusion.2 = f32[640,1280]{1,0:T(8,128)} fusion(bf16[1024,640]{0,1:T(8,128)(2,1)} %mul.117, pred[1024,1280]{0,1:T(32,128)(4,1)S(1)} %eq.120, f32[640,1280]{1,0:T(8,128)} %get-tuple-element.161, pred[]{:T(512)S(6)} %compare.3), kind=kOutput, calls=%fused_computation.1.clone.1 | convolution fusion | flops 1679360000 | bytes 9175041 | tf_op jit(solution)/shard_map/while/body/eval_jaxpr/dot_general | solution.py:60
  33.2 0.8 convolution_reduce_fusion.5
  35.4 1.5 constant_dynamic-slice_fusion.7
  37.4 1.2 mul.117
  38.7 0.9 iota_compare_fusion.4
  40.3 6.0 %convolution_add_fusion.2 = f32[640,1280]{1,0:T(8,128)} fusion(bf16[1024,640]{0,1:T(8,128)(2,1)} %mul.117, pred[1024,1280]{0,1:T(32,128)(4,1)S(1)} %eq.120, f32[640,1280]{1,0:T(8,128)} %get-tuple-element.161, pred[]{:T(512)S(6)} %compare.3), kind=kOutput, calls=%fused_computation.1.clone.1 | convolution fusion | flops 1679360000 | bytes 9175041 | tf_op jit(solution)/shard_map/while/body/eval_jaxpr/dot_general | solution.py:60
  46.4 0.8 convolution_reduce_fusion.5
  48.5 1.5 constant_dynamic-slice_fusion.7
  50.6 1.2 mul.117
  51.8 0.9 iota_compare_fusion.4
  53.5 6.0 %convolution_add_fusion.2 = f32[640,1280]{1,0:T(8,128)} fusion(bf16[1024,640]{0,1:T(8,128)(2,1)} %mul.117, pred[1024,1280]{0,1:T(32,128)(4,1)S(1)} %eq.120, f32[640,1280]{1,0:T(8,128)} %get-tuple-element.161, pred[]{:T(512)S(6)} %compare.3), kind=kOutput, calls=%fused_computation.1.clone.1 | convolution fusion | flops 1679360000 | bytes 9175041 | tf_op jit(solution)/shard_map/while/body/eval_jaxpr/dot_general | solution.py:60
  61.7 1.5 constant_dynamic-slice_fusion.7
  63.8 1.2 mul.117
  65.0 0.9 iota_compare_fusion.4
  66.7 6.0 %convolution_add_fusion.2 = f32[640,1280]{1,0:T(8,128)} fusion(bf16[1024,640]{0,1:T(8,128)(2,1)} %mul.117, pred[1024,1280]{0,1:T(32,128)(4,1)S(1)} %eq.120, f32[640,1280]{1,0:T(8,128)} %get-tuple-element.161, pred[]{:T(512)S(6)} %compare.3), kind=kOutput, calls=%fused_computation.1.clone.1 | convolution fusion | flops 1679360000 | bytes 9175041 | tf_op jit(solution)/shard_map/while/body/eval_jaxpr/dot_general | solution.py:60
  74.9 36.3 %all-reduce = (f32[1280]{0:T(1024)S(1)}, f32[]{:T(128)}, f32[640]{0:T(1024)S(1)}) all-reduce(f32[1280]{0:T(1024)S(1)} %get-tuple-element.46, f32[]{:T(128)} %get-tuple-element.102, f32[640]{0:T(1024)S(1)} %get-tuple-element.45), channel_id=1, replica_groups=mesh['seq'=8,'row'=8,'col'=4] {'seq'}, use_global_device_ids=true, to_apply=%region_6.7 | all-reduce | flops 1921 | bytes 15368 | tf_op jit(solution)/shard_map/psum | solution.py:111
  112.7 51.2 %reduce-scatter.2.cloned.1.call-done = f32[80,1280]{1,0:T(8,128)} async-done(((f32[640,1280]{1,0:T(8,128)}), f32[80,1280]{1,0:T(8,128)}) %reduce-scatter.2.cloned.1.call-update) | async-done | bytes 409616 | tf_op jit(solution)/shard_map/reduce_scatter | solution.py:114
  163.9 1.8 multiply_subtract_fusion
  165.8 10.8 %psum.31 = f32[80,128]{1,0:T(8,128)S(1)} all-reduce(f32[80,128]{1,0:T(8,128)S(1)} %slice_select_fusion), channel_id=1, replica_groups=mesh['seq'=8,'row'=8,'col'=4] {'col'}, use_global_device_ids=true, to_apply=%region_7.8 | all-reduce | flops 10240 | bytes 81920 | tf_op jit(solution)/shard_map/psum | solution.py:15
  176.6 1.7 stack.2
  178.2 10.4 %all-to-all-start = ((f32[64,80,128]{2,1,0:T(8,128)}), f32[64,80,128]{2,1,0:T(8,128)S(1)}, u32[]{:S(2)}, u32[]{:S(2)}) async-start(f32[64,80,128]{2,1,0:T(8,128)} %stack.2), calls=%async_computation.1 | async-start | bytes 5242880 | tf_op jit(solution)/shard_map/all_to_all | solution.py:123
  189.0 62.6 %all-to-all-done = f32[64,80,128]{2,1,0:T(8,128)S(1)} async-done(((f32[64,80,128]{2,1,0:T(8,128)}), f32[64,80,128]{2,1,0:T(8,128)S(1)}, u32[]{:S(2)}, u32[]{:S(2)}) %all-to-all-start) | async-done | bytes 2621472 | tf_op jit(solution)/shard_map/all_to_all | solution.py:123
  251.6 1.6 fusion.3
  (81 shorter events, 14.8 us)
Async XLA Ops:
  6.5 157.4 %reduce-scatter.2.cloned.1.call-start = ((), (), s32[]{:S(2)}) async-start(), calls=%async_computation.2 | async-start | bytes 3686400 | tf_op jit(solution)/shard_map/reduce_scatter | solution.py:114
  14.9 7.5 %copy-start.3 = (s32[4096]{0:T(1024)S(1)}, s32[4096]{0:T(1024)}, u32[]{:S(2)}) copy-start(s32[4096]{0:T(1024)} %param.6) | copy-start | bytes 49156
  23.1 3.3 %copy-start = (s32[4,1024,64]{1,2,0:T(8,128)}, s32[4,1024,64]{1,2,0:T(8,128)S(1)}, u32[]{:S(2)}) copy-start(s32[4,1024,64]{1,2,0:T(8,128)S(1)} %get-tuple-element.175) | copy-start | bytes 3145732 | tf_op jit(solution)/shard_map/while
  33.2 2.1 copy-start.1
  35.3 3.3 %copy-start = (s32[4,1024,64]{1,2,0:T(8,128)}, s32[4,1024,64]{1,2,0:T(8,128)S(1)}, u32[]{:S(2)}) copy-start(s32[4,1024,64]{1,2,0:T(8,128)S(1)} %get-tuple-element.175) | copy-start | bytes 3145732 | tf_op jit(solution)/shard_map/while
  46.4 2.1 copy-start.1
  48.5 3.3 %copy-start = (s32[4,1024,64]{1,2,0:T(8,128)}, s32[4,1024,64]{1,2,0:T(8,128)S(1)}, u32[]{:S(2)}) copy-start(s32[4,1024,64]{1,2,0:T(8,128)S(1)} %get-tuple-element.175) | copy-start | bytes 3145732 | tf_op jit(solution)/shard_map/while
  59.6 2.1 copy-start.1
  61.7 3.3 %copy-start = (s32[4,1024,64]{1,2,0:T(8,128)}, s32[4,1024,64]{1,2,0:T(8,128)S(1)}, u32[]{:S(2)}) copy-start(s32[4,1024,64]{1,2,0:T(8,128)S(1)} %get-tuple-element.175) | copy-start | bytes 3145732 | tf_op jit(solution)/shard_map/while
  72.8 2.1 copy-start.1
  178.2 10.4 %copy-start.2 = (f32[128,128]{1,0:T(8,128)S(1)}, f32[128,128]{1,0:T(8,128)}, u32[]{:S(2)}) copy-start(f32[128,128]{1,0:T(8,128)} %param.7) | copy-start | bytes 196612
  178.2 73.4 %all-to-all-start = ((f32[64,80,128]{2,1,0:T(8,128)}), f32[64,80,128]{2,1,0:T(8,128)S(1)}, u32[]{:S(2)}, u32[]{:S(2)}) async-start(f32[64,80,128]{2,1,0:T(8,128)} %stack.2), calls=%async_computation.1 | async-start | bytes 5242880 | tf_op jit(solution)/shard_map/all_to_all | solution.py:123
Sparse Core Ops, SparseCore 0:
  75.0 88.8 reduce-scatter.1
